TPU v7x, 32 devices: a whole 2x2x4 slice. The times are simulated.
32 devices in a mesh: clip: 8 (over y, x, core), tp: 4 (over z).
Axes of the slice: x: 2, y: 2, z: 4, core: 2. Of those that a mesh axis runs over, the one named last changes fastest.
Arguments:
- patches: bfloat16 [16, 1188, 768], P('clip'), may hold values from -6 to 6
- keep_freq: int32 [16, 12], P('clip'), may hold values from 0 to 1, as said below
- keep_time: int32 [16, 99], P('clip'), may hold values from 0 to 1, as said below
- cotangent: bfloat16 [16, 704, 768], P('clip'), may hold values from -6 to 6
- w_qkv: float32 [768, 3, 768], P(None, None, 'tp'), may hold values from -0.21875 to 0.21875
- w_out: float32 [768, 768], P('tp'), may hold values from -1.5 to 1.5
- w_up: float32 [768, 3072], P(None, 'tp'), may hold values from -0.21875 to 0.21875
- w_down: float32 [3072, 768], P('tp'), may hold values from -0.109375 to 0.109375
- norms: float32 [4, 768], replicated, may hold values from -1 to 1.5
- m_qkv: float32 [768, 3, 768], P('clip', None, 'tp'), may hold values from -256 to 256
- v_qkv: float32 [768, 3, 768], P('clip', None, 'tp'), may hold values from 2008 to 8032
- m_out: float32 [768, 768], P('tp', 'clip'), may hold values from -128 to 128
- v_out: float32 [768, 768], P('tp', 'clip'), may hold values from 385.536 to 1526.08
- m_up: float32 [768, 3072], P('clip', 'tp'), may hold values from -160 to 160
- v_up: float32 [768, 3072], P('clip', 'tp'), may hold values from 722.88 to 2891.52
- m_down: float32 [3072, 768], P('tp', 'clip'), may hold values from -320 to 320
- v_down: float32 [3072, 768], P('tp', 'clip'), may hold values from 3373.44 to 13574.08
- m_norms: float32 [4, 768], P(None, 'clip'), may hold values from -512 to 512
- v_norms: float32 [4, 768], P(None, 'clip'), may hold values from 8032 to 32128
Outputs:
- block_out: bfloat16 [16, 704, 768], P('clip')
- patch_grad: float32 [16, 1188, 768], P('clip')
- norm_grad: float32 [4, 768], P(None, 'clip')
- new_qkv: float32 [768, 3, 768], P(None, None, 'tp')
- new_out: float32 [768, 768], P('tp')
- new_up: float32 [768, 3072], P(None, 'tp')
- new_down: float32 [3072, 768], P('tp')
- new_norms: float32 [4, 768], replicated
- mom1_qkv: float32 [768, 3, 768], P('clip', None, 'tp')
- mom1_out: float32 [768, 768], P('tp', 'clip')
- mom1_up: float32 [768, 3072], P('clip', 'tp')
- mom1_down: float32 [3072, 768], P('tp', 'clip')
- mom1_norms: float32 [4, 768], P(None, 'clip')
- mom2_qkv: float32 [768, 3, 768], P('clip', None, 'tp')
- mom2_out: float32 [768, 768], P('tp', 'clip')
- mom2_up: float32 [768, 3072], P('clip', 'tp')
- mom2_down: float32 [3072, 768], P('tp', 'clip')
- mom2_norms: float32 [4, 768], P(None, 'clip')
- low_qkv: bfloat16 [768, 3, 768], P(None, None, 'tp')
- low_out: bfloat16 [768, 768], P('tp')
- low_up: bfloat16 [768, 3072], P(None, 'tp')
- low_down: bfloat16 [3072, 768], P('tp')
Inputs may be any that keep to these rules, and one draw needn't show every extreme that they name: `keep_freq`: each clip keeps between 4 and 12 frequency bins; its kept bins times kept frames lie between 300 and 704, and in every draw some clip keeps exactly 704 patches. `keep_time`: together with keep_freq, each clip keeps between 300 and 704 patches.
All inputs are finite; a program needn't handle non-finite values.
Results may differ from a plain program's by a relative error of at most 0.014.
The roundings to bfloat16 on the way count: a program that leaves them out, or rounds other values in their place, can miss the bound.
Values sent between devices are 32-bit elements; how exact they have to be, the bound alone decides.
No kernel may reach another device: no remote copies, remote signals or barrier semaphores. Data moves between devices by JAX's collectives and lax.ppermute only.
A program may use at most 128 MiB of HBM per device.

v0:
```python
import jax
import jax.numpy as jnp
from jax import lax
from jax.sharding import PartitionSpec as P

D = 768
HD = 64
FF = 3072
BLOCK = 704
STEP = 3


EPSILON = 1e-06


def positions(keep_freq, keep_time):
    rank_freq = jnp.cumsum(keep_freq, axis=-1) - keep_freq
    rank_time = jnp.cumsum(keep_time, axis=-1) - keep_time
    time_count = jnp.sum(keep_time, axis=-1)
    placed = rank_freq[:, :, None] * time_count[:, None, None] + rank_time[:, None, :]
    present = keep_freq[:, :, None] * keep_time[:, None, :] > 0
    placed = jnp.where(present, placed, -1).reshape(placed.shape[0], -1)
    kept_count = jnp.sum(keep_freq, axis=-1) * time_count
    return (placed, kept_count)


def layer_norm(values, norm_gain, norm_shift):
    centre = values - jnp.mean(values, axis=-1, keepdims=True)
    spread = jnp.mean(centre * centre, axis=-1, keepdims=True)
    return centre * lax.rsqrt(spread + EPSILON) * norm_gain + norm_shift


def gelu_exact(values):
    return jax.nn.gelu(values, approximate=False)


def masked_scores(queries, key_rows, key_live):
    scores = jnp.einsum(
        "jhe,khe->hjk", queries, key_rows, preferred_element_type=jnp.float32
    ) * HD ** (-0.5)
    return jnp.where(key_live[None, None, :], scores, -1000000000.0)


def attend_clip(members):
    queries, key_rows, value_rows, key_live = members
    scores = masked_scores(queries, key_rows, key_live)
    largest = jnp.max(scores, axis=-1, keepdims=True)
    exponent = jnp.exp(scores - largest)
    summed = jnp.sum(exponent, axis=-1, keepdims=True)
    soft_low = (exponent / summed).astype(jnp.bfloat16)
    mixed = jnp.einsum("hjk,khe->jhe", soft_low, value_rows, preferred_element_type=jnp.float32)
    return (mixed.astype(jnp.bfloat16), largest + jnp.log(summed))


def attend_back(members):
    queries, key_rows, value_rows, key_live, log_total, grad_mixed = members
    scores = masked_scores(queries, key_rows, key_live)
    probs = jnp.exp(scores - log_total)
    grad_probs = jnp.einsum(
        "jhe,khe->hjk", grad_mixed, value_rows, preferred_element_type=jnp.float32
    )
    grad_scores = probs * (grad_probs - jnp.sum(grad_probs * probs, axis=-1, keepdims=True))
    scores_low = grad_scores.astype(jnp.bfloat16)
    scale = HD ** (-0.5)
    grad_query = (
        jnp.einsum("hjk,khe->jhe", scores_low, key_rows, preferred_element_type=jnp.float32) * scale
    )
    grad_key = (
        jnp.einsum("hjk,jhe->khe", scores_low, queries, preferred_element_type=jnp.float32) * scale
    )
    grad_value = jnp.einsum(
        "hjk,jhe->khe", probs.astype(jnp.bfloat16), grad_mixed, preferred_element_type=jnp.float32
    )
    return jnp.stack([grad_query, grad_key, grad_value], axis=1).astype(jnp.bfloat16)


def own_part(array, axis_dim, clip_index, parts):
    part_width = array.shape[axis_dim] // parts
    return lax.dynamic_slice_in_dim(array, clip_index * part_width, part_width, axis_dim)


def adam_step(weight, gradient, first_mom, second_mom, rate):
    first_new = 0.5 * first_mom + 0.5 * gradient
    second_new = 0.5 * second_mom + 0.5 * gradient * gradient
    fix = 1.0 - 0.5**STEP
    direction = first_new / fix / (jnp.sqrt(second_new / fix) + 1e-08)
    return (weight - rate * (direction + 0.01 * weight), first_new, second_new)


def on_device(
    patches,
    keep_freq,
    keep_time,
    cotangent,
    w_qkv,
    w_out,
    w_up,
    w_down,
    norms,
    m_qkv,
    v_qkv,
    m_out,
    v_out,
    m_up,
    v_up,
    m_down,
    v_down,
    m_norms,
    v_norms,
):
    clip_count, block_len, model_width = cotangent.shape
    row_count = clip_count * block_len
    local_width = w_qkv.shape[2]
    heads_dev = local_width // HD
    placed, kept_count = positions(keep_freq, keep_time)
    slot_ids = jnp.arange(block_len, dtype=jnp.int32)
    select = (placed[:, None, :] == slot_ids[None, :, None]).astype(jnp.bfloat16)
    key_live = slot_ids[None, :] < kept_count[:, None]
    row_live = key_live.astype(jnp.float32).reshape(row_count, 1)
    qkv_low = w_qkv.astype(jnp.bfloat16)
    out_low = w_out.astype(jnp.bfloat16)
    up_low = w_up.astype(jnp.bfloat16)
    down_low = w_down.astype(jnp.bfloat16)
    inputs = jnp.einsum(
        "cjp,cpd->cjd", select, patches, preferred_element_type=jnp.float32
    ).reshape(row_count, model_width)
    first_low = layer_norm(inputs, norms[0], norms[1]).astype(jnp.bfloat16)
    packed = jnp.einsum(
        "rd,dke->rke", first_low, qkv_low, preferred_element_type=jnp.float32
    ).astype(jnp.bfloat16)
    unpacked = packed.reshape(clip_count, block_len, 3, heads_dev, HD)
    queries = unpacked[:, :, 0]
    key_rows = unpacked[:, :, 1]
    value_rows = unpacked[:, :, 2]
    mixed, log_total = lax.map(attend_clip, (queries, key_rows, value_rows, key_live))
    mixed_rows = mixed.reshape(row_count, local_width)
    attn = lax.psum(jnp.dot(mixed_rows, out_low, preferred_element_type=jnp.float32), "tp")
    middle = inputs + attn
    second_low = layer_norm(middle, norms[2], norms[3]).astype(jnp.bfloat16)
    hidden = jnp.dot(second_low, up_low, preferred_element_type=jnp.float32)
    active_low = gelu_exact(hidden).astype(jnp.bfloat16)
    branch = lax.psum(jnp.dot(active_low, down_low, preferred_element_type=jnp.float32), "tp")
    result = (middle + branch) * row_live
    block_out = result.astype(jnp.bfloat16).reshape(clip_count, block_len, model_width)
    grad_result = cotangent.reshape(row_count, model_width).astype(jnp.float32) * row_live
    result_low = grad_result.astype(jnp.bfloat16)
    grad_down = jnp.einsum("rf,rd->fd", active_low, result_low, preferred_element_type=jnp.float32)
    grad_active = jnp.einsum("rd,fd->rf", result_low, down_low, preferred_element_type=jnp.float32)
    gelu_pull = jax.vjp(gelu_exact, hidden)[1]
    hidden_low = gelu_pull(grad_active)[0].astype(jnp.bfloat16)
    grad_up = jnp.einsum("rd,rf->df", second_low, hidden_low, preferred_element_type=jnp.float32)
    grad_second = lax.psum(
        jnp.einsum("rf,df->rd", hidden_low, up_low, preferred_element_type=jnp.float32), "tp"
    )
    second_pull = jax.vjp(layer_norm, middle, norms[2], norms[3])[1]
    grad_mid_norm, grad_gain2, grad_shift2 = second_pull(grad_second)
    grad_middle = grad_result + grad_mid_norm
    middle_low = grad_middle.astype(jnp.bfloat16)
    grad_out = jnp.einsum("rf,rd->fd", mixed_rows, middle_low, preferred_element_type=jnp.float32)
    grad_mixed = jnp.einsum("rd,fd->rf", middle_low, out_low, preferred_element_type=jnp.float32)
    grad_mixed = grad_mixed.astype(jnp.bfloat16).reshape(clip_count, block_len, heads_dev, HD)
    grad_packed = lax.map(
        attend_back, (queries, key_rows, value_rows, key_live, log_total, grad_mixed)
    )
    grad_packed = grad_packed.reshape(row_count, 3, local_width)
    grad_qkv = jnp.einsum("rd,rke->dke", first_low, grad_packed, preferred_element_type=jnp.float32)
    grad_first = lax.psum(
        jnp.einsum("rke,dke->rd", grad_packed, qkv_low, preferred_element_type=jnp.float32), "tp"
    )
    first_pull = jax.vjp(layer_norm, inputs, norms[0], norms[1])[1]
    grad_in_norm, grad_gain1, grad_shift1 = first_pull(grad_first)
    inputs_low = (
        (grad_middle + grad_in_norm)
        .astype(jnp.bfloat16)
        .reshape(clip_count, block_len, model_width)
    )
    patch_grad = jnp.einsum("cjp,cjd->cpd", select, inputs_low, preferred_element_type=jnp.float32)
    grad_norms = jnp.stack([grad_gain1, grad_shift1, grad_gain2, grad_shift2])
    clip_index = lax.axis_index("clip")
    parts = lax.axis_size("clip")
    summed = lax.psum((grad_qkv, grad_out, grad_up, grad_down, grad_norms), "clip")
    piece_qkv = own_part(summed[0], 0, clip_index, parts)
    piece_out = own_part(summed[1], 1, clip_index, parts)
    piece_up = own_part(summed[2], 0, clip_index, parts)
    piece_down = own_part(summed[3], 1, clip_index, parts)
    piece_norms = own_part(summed[4], 1, clip_index, parts)
    rate_model = D ** (-0.5)
    qkv_new = adam_step(own_part(w_qkv, 0, clip_index, parts), piece_qkv, m_qkv, v_qkv, rate_model)
    out_new = adam_step(
        own_part(w_out, 1, clip_index, parts),
        piece_out,
        m_out,
        v_out,
        max(16 * D // BLOCK, 1) ** (-0.5),
    )
    up_new = adam_step(own_part(w_up, 0, clip_index, parts), piece_up, m_up, v_up, rate_model)
    down_new = adam_step(
        own_part(w_down, 1, clip_index, parts), piece_down, m_down, v_down, FF ** (-0.5)
    )
    norms_new = adam_step(own_part(norms, 1, clip_index, parts), piece_norms, m_norms, v_norms, 0.3)
    full_qkv, full_out, full_up, full_down, full_norms = (
        lax.all_gather(qkv_new[0], "clip", axis=0, tiled=True),
        lax.all_gather(out_new[0], "clip", axis=1, tiled=True),
        lax.all_gather(up_new[0], "clip", axis=0, tiled=True),
        lax.all_gather(down_new[0], "clip", axis=1, tiled=True),
        lax.all_gather(norms_new[0], "clip", axis=1, tiled=True),
    )
    return (
        block_out,
        patch_grad,
        piece_norms,
        full_qkv,
        full_out,
        full_up,
        full_down,
        full_norms,
        qkv_new[1],
        out_new[1],
        up_new[1],
        down_new[1],
        norms_new[1],
        qkv_new[2],
        out_new[2],
        up_new[2],
        down_new[2],
        norms_new[2],
        full_qkv.astype(jnp.bfloat16),
        full_out.astype(jnp.bfloat16),
        full_up.astype(jnp.bfloat16),
        full_down.astype(jnp.bfloat16),
    )


def solution(mesh):
    return jax.shard_map(
        on_device,
        mesh=mesh,
        in_specs=(
            P("clip", None, None),
            P("clip", None),
            P("clip", None),
            P("clip", None, None),
            P(None, None, "tp"),
            P("tp", None),
            P(None, "tp"),
            P("tp", None),
            P(),
            P("clip", None, "tp"),
            P("clip", None, "tp"),
            P("tp", "clip"),
            P("tp", "clip"),
            P("clip", "tp"),
            P("clip", "tp"),
            P("tp", "clip"),
            P("tp", "clip"),
            P(None, "clip"),
            P(None, "clip"),
        ),
        out_specs=(
            P("clip", None, None),
            P("clip", None, None),
            P(None, "clip"),
            P(None, None, "tp"),
            P("tp", None),
            P(None, "tp"),
            P("tp", None),
            P(),
            P("clip", None, "tp"),
            P("tp", "clip"),
            P("clip", "tp"),
            P("tp", "clip"),
            P(None, "clip"),
            P("clip", None, "tp"),
            P("tp", "clip"),
            P("clip", "tp"),
            P("tp", "clip"),
            P(None, "clip"),
            P(None, None, "tp"),
            P("tp", None),
            P(None, "tp"),
            P("tp", None),
        ),
        check_vma=False,
    )
```

profile of v0, /device:TPU:0, one launch (start us, length us, event | category | flops | bytes accessed | tf_op | source)
XLA Modules:
  0.0 1050.1 jit_solution(1938424394825000828)
XLA Ops:
  15.1 7.1 fusion.101
  32.2 4.6 reshape.318
  38.3 11.0 %while.22 = (s32[]{:T(128)}, bf16[2,704,3,64]{1,3,2,0:T(8,128)(2,1)}, f32[2,3,704,1]{2,1,3,0:T(4,128)S(1)}, bf16[2,704,3,64]{1,3,2,0:T(8,128)(2,1)S(1)}, pred[2,...) while((s32[]{:T(128)}, ...), condition=%wide.region_9.10_spmd, body=%wide.region_6.9_spmd.sunk | while | flops 398608320 | bytes 23981020 | solution.py:135
  52.4 4.2 fusion.82
  58.8 160.0 %all-reduce.7.cloned.1.call-done = f32[1408,768]{1,0:T(8,128)} async-done(((f32[1408,768]{1,0:T(8,128)}), f32[1408,768]{1,0:T(8,128)}) %all-reduce.7.cloned.1.call-update) | async-done | bytes 4325392 | tf_op jit(solution)/shard_map/psum | solution.py:137
  218.8 4.1 fusion.97
  226.0 11.7 %multiply_convert_fusion.2 = (bf16[1408,768]{1,0:T(8,128)(2,1)}, f32[1408,768]{1,0:T(8,128)S(1)}, f32[1408,768]{1,0:T(8,128)S(1)}) fusion(bf16[1408,768]{1,0:T(8,128)(2,1)S(1)} %add_convert_fusion.3, f32[768,768]{1,0:T(8,128)S(1)} %copy-done.35), kind=kOutput, calls=%fused_computation.82 | convolution fusion | flops 1731821568 | bytes 15335424 | tf_op jit(solution)/shard_map/dot_general | solution.py:140
  242.3 4.0 fusion.74
  246.8 3.8 add_convert_fusion
  251.1 3.5 fusion.105
  254.5 3.5 fusion.106
  258.0 146.7 %all-reduce.9.cloned.1.call-done = f32[1408,768]{1,0:T(8,128)} async-done(((f32[1408,768]{1,0:T(8,128)}), f32[1408,768]{1,0:T(8,128)}) %all-reduce.9.cloned.1.call-update) | async-done | bytes 4325392 | tf_op jit(solution)/shard_map/psum | solution.py:152
  404.7 5.2 multiply_reduce_fusion.1
  409.9 3.7 fusion.95
  423.6 20.4 %while.23 = (s32[]{:T(128)}, bf16[2,704,3,3,64]{1,4,3,2,0:T(8,128)(2,1)}, bf16[2,704,3,64]{1,3,2,0:T(8,128)(2,1)S(1)}, pred[2,704]{1,0:T(4,128)(4,1)S(1)}, bf16[...) while((s32[]{:T(128)}, ...), condition=%wide.region_19.20_spmd, body=%wide.region_17.19_spmd.sunk | while | flops 976992192 | bytes 68247088 | solution.py:162
  444.0 4.5 copy.88
  448.5 5.0 reshape.322
  453.5 5.5 fusion.103
  460.5 117.8 %all-reduce.11.cloned.1.call-done = (f32[768,3,192]{2,0,1:T(8,128)}, f32[192,768]{1,0:T(8,128)}, f32[768,768]{1,0:T(8,128)}, f32[768,768]{0,1:T(8,128)}) async-done(((f32[768,3,192]{2,0,1:T(8,128)}, f32[192,768]{1,0:T(8,128)}, f32[768,768]{1,0:T(8,128)}, f32[768,768]{0,1:T(8,128)}), (f32[768,3,192]{2,0,1:T(8,128)}, f32[192,768]{1,0:T(8,128)}, f32[768,768]{1,0:T(8,128)}, ...) | async-done | bytes 7077904 | tf_op jit(solution)/shard_map/psum | solution.py:181
  586.6 6.5 fusion.70
  593.1 4.0 convolution_bitcast_fusion
  599.9 12.2 %all_gather.16 = f32[192,768]{0,1:T(8,128)S(1)} all-gather(f32[192,96]{0,1:T(8,128)S(1)} %copy.91), channel_id=1, replica_groups=mesh['clip'=8,'tp'=4] {'clip'}, dimensions={1}, use_global_device_ids=true | all-gather | bytes 663552 | tf_op jit(solution)/shard_map/all_gather | solution.py:203
  620.2 23.5 %all-gather.9.cloned.1.call-done = f32[768,768]{0,1:T(8,128)} async-done(((f32[768,96]{0,1:T(8,128)}), f32[768,768]{0,1:T(8,128)}) %all-gather.9.cloned.1.call-update) | async-done | bytes 2359312 | tf_op jit(solution)/shard_map/all_gather | solution.py:205
  646.9 28.1 %all-gather.7.cloned.1.call-done = f32[768,768]{1,0:T(8,128)} async-done(((f32[96,768]{1,0:T(8,128)}), f32[768,768]{1,0:T(8,128)}) %all-gather.7.cloned.1.call-update) | async-done | bytes 2359312 | tf_op jit(solution)/shard_map/all_gather | solution.py:204
  680.9 296.8 %all-reduce.13.cloned.1.call-done = (f32[1408,768]{1,0:T(8,128)}, f32[1408,768]{1,0:T(8,128)}) async-done(((f32[1408,768]{1,0:T(8,128)}, f32[1408,768]{1,0:T(8,128)}), (f32[1408,768]{1,0:T(8,128)}, f32[1408,768]{1,0:T(8,128)})) %all-reduce.13.cloned.1.call-update) | async-done | bytes 8650768 | tf_op jit(solution)/shard_map/psum | solution.py:142
  977.6 5.2 multiply_reduce_fusion.2
  983.7 3.4 fusion.94
  987.1 24.0 %psum.67 = f32[4,768]{1,0:T(4,128)S(1)} all-reduce(f32[4,768]{1,0:T(4,128)S(1)} %pad_maximum_fusion), channel_id=1, replica_groups=mesh['clip'=8,'tp'=4] {'clip'}, use_global_device_ids=true, to_apply=%region_27.28 | all-reduce | flops 3072 | bytes 24576 | tf_op jit(solution)/shard_map/psum | solution.py:181
  1012.5 8.2 all-gather
  1021.4 8.1 add_convert_fusion.1
  1029.5 3.5 fusion.54
  1033.0 8.6 copy.94
  (213 shorter events, 108.0 us)
Async XLA Ops:
  7.2 211.6 %all-reduce.7.cloned.1.call-start = ((), (), s32[]{:S(2)}) async-start(), calls=%async_computation | async-start | bytes 8650752 | tf_op jit(solution)/shard_map/psum | solution.py:137
  11.7 10.4 copy-start.36
  22.2 5.9 copy-start.26
  25.1 5.7 copy-start.32
  52.4 4.6 copy-start.2
  56.6 348.1 %all-reduce.9.cloned.1.call-start = ((), (), s32[]{:S(2)}) async-start(), calls=%async_computation.1 | async-start | bytes 8650752 | tf_op jit(solution)/shard_map/psum | solution.py:152
  226.0 11.8 %copy-start.6 = (bf16[1408,768]{1,0:T(8,128)(2,1)}, bf16[1408,768]{1,0:T(8,128)(2,1)S(1)}, u32[]{:S(2)}) copy-start(bf16[1408,768]{1,0:T(8,128)(2,1)S(1)} %add_convert_fusion.3) | copy-start | bytes 6488068
  226.0 11.8 %copy-start.15 = (bf16[1408,768]{1,0:T(8,128)(2,1)S(1)}, bf16[1408,768]{1,0:T(8,128)(2,1)}, u32[]{:S(2)}) copy-start(bf16[1408,768]{1,0:T(8,128)(2,1)} %fusion.58) | copy-start | bytes 6488068
  226.0 11.8 %copy-start.34 = (f32[768,768]{1,0:T(8,128)S(1)}, f32[768,768]{1,0:T(8,128)}, u32[]{:S(2)}) copy-start(f32[768,768]{1,0:T(8,128)} %param.30) | copy-start | bytes 7077892
  246.3 331.9 %all-reduce.11.cloned.1.call-start = ((), (), s32[]{:S(2)}) async-start(), calls=%async_computation.5 | async-start | bytes 15335424 | tf_op jit(solution)/shard_map/psum | solution.py:181
  246.8 3.9 copy-start.7
  246.8 4.3 copy-start.14
  404.7 5.2 copy-start.4
  459.0 119.3 %copy-start.23 = (f32[96,3,192]{2,0,1:T(8,128)S(1)}, f32[96,3,192]{2,0,1:T(8,128)}, u32[]{:S(2)}) copy-start(f32[96,3,192]{2,0,1:T(8,128)} %param.32) | copy-start | bytes 663556
  459.0 119.3 %copy-start.24 = (f32[96,3,192]{2,0,1:T(8,128)S(1)}, f32[96,3,192]{2,0,1:T(8,128)}, u32[]{:S(2)}) copy-start(f32[96,3,192]{2,0,1:T(8,128)} %param.33) | copy-start | bytes 663556
  459.0 155.1 %all-gather.5.cloned.1.call-start = ((), (), s32[]{:S(2)}) async-start(), calls=%async_computation.2 | async-start | bytes 2654208 | tf_op jit(solution)/shard_map/all_gather | solution.py:202
  580.3 4.0 copy-start.25
  580.3 63.3 %all-gather.9.cloned.1.call-start = ((), (), s32[]{:S(2)}) async-start(), calls=%async_computation.4 | async-start | bytes 2654208 | tf_op jit(solution)/shard_map/all_gather | solution.py:205
  584.3 90.7 %all-gather.7.cloned.1.call-start = ((), (), s32[]{:S(2)}) async-start(), calls=%async_computation.3 | async-start | bytes 2654208 | tf_op jit(solution)/shard_map/all_gather | solution.py:204
  586.5 6.6 copy-start.20
  586.5 391.1 %all-reduce.13.cloned.1.call-start = ((), (), s32[]{:S(2)}) async-start(), calls=%async_computation.6 | async-start | bytes 17301504 | tf_op jit(solution)/shard_map/psum | solution.py:142
  586.6 6.5 copy-start.19
  646.9 330.8 %copy-start.27 = (f32[1408]{0:T(1024)S(1)}, f32[1408]{0:T(1024)}, u32[]{:S(2)}) copy-start(f32[1408]{0:T(1024)} %copy-done.26) | copy-start | bytes 16900
  646.9 330.8 %copy-start.29 = (f32[1408]{0:T(1024)S(1)}, f32[1408]{0:T(1024)}, u32[]{:S(2)}) copy-start(f32[1408]{0:T(1024)} %copy-done.28) | copy-start | bytes 16900
  675.0 307.8 %slice-start = ((s8[4325376]{0:T(1024)(128)(4,1)}), s8[131072]{0:T(1024)(128)(4,1)S(1)}, s32[]{:S(2)}) async-start(s8[4325376]{0:T(1024)(128)(4,1)} %bitcast.163), calls=%async_computation.7 | async-start | bytes 262144
  977.6 5.2 copy-start.33
  977.6 5.2 slice-start.1
  977.6 6.0 copy-start.3
  983.7 27.5 %copy-start.38 = (f32[4,96]{1,0:T(4,128)S(1)}, f32[4,96]{1,0:T(4,128)}, u32[]{:S(2)}) copy-start(f32[4,96]{1,0:T(4,128)} %param.40) | copy-start | bytes 4612
  983.7 27.5 %copy-start.39 = (f32[4,96]{1,0:T(4,128)S(1)}, f32[4,96]{1,0:T(4,128)}, u32[]{:S(2)}) copy-start(f32[4,96]{1,0:T(4,128)} %param.41) | copy-start | bytes 4612
  1021.4 8.1 copy-start.37
  1033.0 8.6 copy-start.5
  (24 other events, 43.0 us)
Sparse Core Ops, SparseCore 0:
  56.7 161.9 all-reduce.6
  246.4 158.2 all-reduce.8
  459.1 119.0 all-reduce.10
  580.6 31.3 all-gather.4
  614.2 29.3 all-gather.8
  645.9 29.0 all-gather.6
  677.6 299.9 all-reduce.12
where the time goes:
time: 1050 us
  waiting for transfers between devices  773 us (74%)
  matrix products  81.6 us (8%)
  other arithmetic  75.4 us (7%)
  local copies, waits for them, and re-layouts  59.3 us (6%)
  blocking collectives  44.5 us (4%)
  between operations  14.9 us (1%)
    psum x1, waiting for transfers between devices, on_device(): lax.psum(jnp.dot(active_low, down_low, preferred_element_type=jnp.float32...  297 us
    psum x1, waiting for transfers between devices, on_device(): lax.psum(jnp.dot(mixed_rows, out_low, preferred_element_type=jnp.float32)...  160 us
    psum x1, waiting for transfers between devices, on_device(): lax.psum(jnp.einsum('rf,df->rd', hidden_low, up_low, preferred_element_ty...  147 us
    psum x1, waiting for transfers between devices, on_device(): lax.psum((grad_qkv, grad_out, grad_up, grad_down, grad_norms), 'clip')  118 us
    all_gather x1, waiting for transfers between devices, on_device(): lax.all_gather(up_new[0], 'clip', axis=0, tiled=True)  28.1 us
    unnamed x86, local copies, waits for them, and re-layouts  27.8 us
    psum x1, blocking collectives, on_device(): lax.psum((grad_qkv, grad_out, grad_up, grad_down, grad_norms), 'clip')  24 us
    all_gather x1, waiting for transfers between devices, on_device(): lax.all_gather(down_new[0], 'clip', axis=1, tiled=True)  23.5 us
  transfers between devices with their start and end apart: 7, of which 6 were waited for; matrix products, arithmetic and copies ran while one was open for 5% of the time, Pallas kernels for 0%

commit v1 on v0

v1 whole, which is shorter than its diff:
```python
import functools

import jax
import jax.numpy as jnp
from jax import lax
from jax.experimental import pallas as pl
from jax.experimental.pallas import tpu as pltpu
from jax.sharding import PartitionSpec as P

D = 768
HD = 64
FF = 3072
BLOCK = 704
STEP = 3
EPSILON = 1e-06
SCALE = HD ** (-0.5)
GROUP = 8
F32 = jnp.float32
BF16 = jnp.bfloat16
VMEM_LIMIT = 56 * 2**20


def dot(left, right, left_dim, right_dim):
    return lax.dot_general(
        left, right, (((left_dim,), (right_dim,)), ((), ())), preferred_element_type=F32
    )


def positions(keep_freq, keep_time):
    rank_freq = jnp.cumsum(keep_freq, axis=-1) - keep_freq
    rank_time = jnp.cumsum(keep_time, axis=-1) - keep_time
    time_count = jnp.sum(keep_time, axis=-1)
    placed = rank_freq[:, :, None] * time_count[:, None, None] + rank_time[:, None, :]
    present = keep_freq[:, :, None] * keep_time[:, None, :] > 0
    placed = jnp.where(present, placed, -1).reshape(placed.shape[0], -1)
    kept_count = jnp.sum(keep_freq, axis=-1) * time_count
    return (placed, kept_count)


def norm_parts(values):
    centre = values - jnp.mean(values, axis=-1, keepdims=True)
    spread = jnp.mean(centre * centre, axis=-1, keepdims=True)
    inverse = lax.rsqrt(spread + EPSILON)
    return centre * inverse, inverse


def norm_back(values, gain, grad):
    unit, inverse = norm_parts(values)
    grad_unit = grad * gain
    mean_grad = jnp.mean(grad_unit, axis=-1, keepdims=True)
    mean_both = jnp.mean(grad_unit * unit, axis=-1, keepdims=True)
    back = inverse * (grad_unit - mean_grad - unit * mean_both)
    gain_grad = jnp.sum(grad * unit, axis=0, keepdims=True)
    shift_grad = jnp.sum(grad, axis=0, keepdims=True)
    return back, gain_grad, shift_grad


def live_column(kept, length):
    return lax.broadcasted_iota(jnp.int32, (length, 1), 0) < kept


def tree_sum(parts, odd):
    if len(parts) != 4:
        total = parts[0]
        for part in parts[1:]:
            total = total + part
        return total
    own, after, across, before = parts
    near = jnp.where(odd, before, after)
    far = jnp.where(odd, after, before)
    return (own + near) + (across + far)


def call(body, grid, in_specs, out_specs, out_shape, scratch=(), scalars=2, aliases=None, cost=None):
    return pl.pallas_call(
        body,
        grid_spec=pltpu.PrefetchScalarGridSpec(
            num_scalar_prefetch=scalars,
            grid=grid,
            in_specs=in_specs,
            out_specs=out_specs,
            scratch_shapes=list(scratch),
        ),
        out_shape=out_shape,
        input_output_aliases=aliases or {},
        compiler_params=pltpu.CompilerParams(
            dimension_semantics=("arbitrary",) * len(grid), vmem_limit_bytes=VMEM_LIMIT
        ),
        cost_estimate=pl.CostEstimate(flops=cost[0], bytes_accessed=cost[1], transcendentals=0)
        if cost
        else None,
    )


def clip_block(*dims):
    return pl.BlockSpec((1, *dims), lambda c, *_: (c,) + (0,) * len(dims))


def whole_block(*dims):
    return pl.BlockSpec(dims, lambda *_: (0,) * len(dims))


ANY = pl.BlockSpec(memory_space=pl.ANY)


def front_kernel(kept, order, placed, patches, cot, norms, inputs, first, grad):
    clip = pl.program_id(0)
    length, patch_count = first.shape[1], placed.shape[2]
    slots = lax.broadcasted_iota(jnp.int32, (length, patch_count), 0)
    select = jnp.where(placed[0] == slots, 1.0, 0.0).astype(BF16)
    picked = dot(select, patches[0], 1, 0)
    inputs[0] = picked
    unit, _ = norm_parts(picked)
    first[0] = (unit * norms[0:1] + norms[1:2]).astype(BF16)
    live = live_column(kept[clip], length)
    grad[0] = jnp.where(live, cot[0].astype(F32), 0.0).astype(BF16)


def piece_copies(order, sources, start, rows, target, sems):
    near, far = sources
    copies = []
    for slot in range(GROUP):
        source = (near if slot < GROUP // 2 else far).at[slot % (GROUP // 2), pl.ds(start, rows)]
        place = pl.multiple_of(order[slot] * rows, 8)
        copies.append(
            pltpu.make_async_copy(source, target.at[pl.ds(place, rows)], sems.at[slot])
        )
    return copies


def augment(rows, extra_row, length):
    index = lax.broadcasted_iota(jnp.int32, (16, length), 0)
    extra = jnp.where(index == 0, extra_row, 0.0).astype(BF16)
    return jnp.concatenate([rows, extra], axis=0)


def key_bias(kept, length):
    slot = lax.broadcasted_iota(jnp.int32, (1, length), 1)
    return jnp.where(slot < kept, 0.0, -1000000000.0)


def attend_kernel(own, heads, kept, order, first, *refs):
    clip = pl.program_id(0)
    if own:
        source, packed, mixed, total, low = refs

        @pl.when(clip == 0)
        def _():
            low[...] = source[...].astype(BF16)
    else:
        near, far, packed, mixed, total, low, staged, sems = refs

        @pl.when(clip == 0)
        def _():
            copies = piece_copies(order, (near, far), 0, low.shape[0] // GROUP, staged, sems)
            for copy in copies:
                copy.start()
            for copy in copies:
                copy.wait()
            low[...] = staged[...].astype(BF16)

    length = first.shape[1]
    width = heads * HD
    rows = dot(low[...], first[0], 1, 1).astype(BF16)
    packed[0] = rows
    bias = key_bias(kept[clip], length)
    ones = jnp.ones((1, length), F32)
    for head in range(heads):
        at = head * HD
        query = augment((rows[at : at + HD] * SCALE).astype(BF16), ones, length)
        key = augment(rows[width + at : width + at + HD], bias, length)
        value = rows[2 * width + at : 2 * width + at + HD]
        scores = dot(key, query, 0, 0)
        largest = jnp.max(scores, axis=0, keepdims=True)
        exponent = jnp.exp(scores - largest)
        summed = jnp.sum(exponent, axis=0, keepdims=True)
        mix = dot(value, exponent.astype(BF16), 1, 0) / summed
        mixed[0, at : at + HD] = mix.astype(BF16)
        total[0, head : head + 1] = largest + jnp.log(summed)


def project_kernel(shards, kept, order, *refs):
    clip = pl.program_id(0)
    inputs, norms, source = refs[:3]
    pieces = refs[3 : 3 + 2 * (shards - 1)]
    mixes = refs[3 + 2 * (shards - 1) : 3 + 2 * (shards - 1) + shards]
    middle, second, low, staged, sems = refs[3 + 2 * (shards - 1) + shards :]

    @pl.when(clip == 0)
    def _():
        copies = []
        for shard in range(shards - 1):
            copies += piece_copies(
                order,
                pieces[2 * shard : 2 * shard + 2],
                0,
                low.shape[1] // GROUP,
                staged.at[shard],
                sems.at[shard],
            )
        for copy in copies:
            copy.start()
        low[0] = source[...].astype(BF16)
        for copy in copies:
            copy.wait()
        for shard in range(shards - 1):
            low[shard + 1] = staged[shard].astype(BF16)

    odd = order[GROUP] > 0
    parts = [dot(mixes[shard][0], low[shard], 0, 0) for shard in range(shards)]
    values = inputs[0] + tree_sum(parts, odd)
    middle[0] = values
    unit, _ = norm_parts(values)
    second[0] = (unit * norms[2:3] + norms[3:4]).astype(BF16)


HALF_ROOT = 0.7071067811865476
DENSITY = 0.3989422804014327


def mlp_kernel(own, chunk, kept, order, second, grad, *refs):
    clip = pl.program_id(0)
    if own:
        up_source, down_source, branch, back, up_grad, down_grad, up_low, down_low = refs

        @pl.when(clip == 0)
        def _():
            up_low[...] = up_source[...].astype(BF16)
            down_low[...] = down_source[...].astype(BF16)
            up_grad[...] = jnp.zeros_like(up_grad)
            down_grad[...] = jnp.zeros_like(down_grad)
    else:
        near, far, branch, back, up_low, down_low, staged, sems = refs

        @pl.when(clip == 0)
        def _():
            rows = up_low.shape[0] // GROUP
            skip = near.shape[1] - 2 * rows
            copies = []
            for index in range(2):
                copies += piece_copies(
                    order, (near, far), skip + index * rows, rows, staged.at[index], sems.at[index]
                )
            for copy in copies:
                copy.start()
            for copy in copies:
                copy.wait()
            up_low[...] = staged[0].astype(BF16)
            down_low[...] = staged[1].astype(BF16)

    rows = second[0]
    upstream = grad[0]
    branch_sum = None
    for start in range(0, up_low.shape[1], chunk):
        up = up_low[:, start : start + chunk]
        down = down_low[start : start + chunk]
        hidden = dot(rows, up, 1, 0)
        grad_active = dot(upstream, down, 1, 1)
        cumulative = 0.5 * (lax.erf(hidden * HALF_ROOT) + 1.0)
        active = (hidden * cumulative).astype(BF16)
        slope = cumulative + hidden * (DENSITY * jnp.exp(-0.5 * hidden * hidden))
        grad_hidden = (slope * grad_active).astype(BF16)
        branch_part = dot(active, down, 1, 0)
        back_part = dot(grad_hidden, up, 1, 1)
        branch_sum = branch_part if branch_sum is None else branch_sum + branch_part
        back_sum = back_part if start == 0 else back_sum + back_part
        if own:
            up_grad[:, start : start + chunk] += dot(rows, grad_hidden, 0, 0)
            down_grad[:, start : start + chunk] += dot(upstream, active, 0, 0)
    branch[0] = branch_sum
    back[0] = back_sum


def close_kernel(shards, kept, order, *refs):
    clip = pl.program_id(0)
    middle, grad, norms = refs[:3]
    branches = refs[3 : 3 + shards]
    backs = refs[3 + shards : 3 + 2 * shards]
    result, grad_middle, low, norm_grad = refs[3 + 2 * shards :]
    odd = order[GROUP] > 0
    live = live_column(kept[clip], middle.shape[1])
    values = middle[0]
    total = values + tree_sum([ref[0] for ref in branches], odd)
    result[0] = jnp.where(live, total, 0.0).astype(BF16)
    back, gain_grad, shift_grad = norm_back(
        values, norms[2:3], tree_sum([ref[0] for ref in backs], odd)
    )
    both = grad[0].astype(F32) + back
    grad_middle[0] = both
    low[0] = both.astype(BF16)

    @pl.when(clip == 0)
    def _():
        norm_grad[...] = jnp.zeros_like(norm_grad)

    norm_grad[0:1] += gain_grad
    norm_grad[1:2] += shift_grad


def attend_back_kernel(own, heads, kept, order, packed, mixed, total, grad, out_low, *refs):
    clip = pl.program_id(0)
    if own:
        first, grad_packed, qkv_grad, out_grad = refs
    else:
        (grad_packed,) = refs
    length = grad.shape[1]
    width = heads * HD
    grad_mixed = dot(out_low[0], grad[0], 1, 1).astype(BF16)
    bias = key_bias(kept[clip], length)
    ones = jnp.ones((1, length), F32)
    for head in range(heads):
        at = head * HD
        query_low = (packed[0, at : at + HD] * SCALE).astype(BF16)
        key_low = packed[0, width + at : width + at + HD]
        value = packed[0, 2 * width + at : 2 * width + at + HD]
        query = augment(query_low, ones, length)
        key = augment(key_low, bias, length)
        upstream = grad_mixed[at : at + HD]
        offset = jnp.sum(
            upstream.astype(F32) * mixed[0, at : at + HD].astype(F32), axis=0, keepdims=True
        )
        probs = jnp.exp(dot(key, query, 0, 0) - total[0, head : head + 1])
        grad_probs = dot(value, upstream, 0, 0)
        scores_low = (probs * (grad_probs - offset)).astype(BF16)
        probs_low = probs.astype(BF16)
        grad_packed[0, at : at + HD] = (dot(key_low, scores_low, 1, 0) * SCALE).astype(BF16)
        grad_packed[0, width + at : width + at + HD] = dot(query_low, scores_low, 1, 1).astype(BF16)
        grad_packed[0, 2 * width + at : 2 * width + at + HD] = dot(
            upstream, probs_low, 1, 1
        ).astype(BF16)
    if own:

        @pl.when(clip == 0)
        def _():
            qkv_grad[...] = jnp.zeros_like(qkv_grad)
            out_grad[...] = jnp.zeros_like(out_grad)

        qkv_grad[...] += dot(first[0], grad_packed[0], 0, 1)
        out_grad[...] += dot(grad[0], mixed[0], 0, 1)


def final_kernel(shards, kept, order, *refs):
    clip = pl.program_id(0)
    placed, inputs, grad_middle, norms = refs[:4]
    packs = refs[4 : 4 + shards]
    lows = refs[4 + shards : 4 + 2 * shards]
    patch_grad, norm_grad = refs[4 + 2 * shards :]
    odd = order[GROUP] > 0
    parts = [dot(packs[shard][0], lows[shard][...], 0, 0) for shard in range(shards)]
    back, gain_grad, shift_grad = norm_back(inputs[0], norms[0:1], tree_sum(parts, odd))
    low = (grad_middle[0] + back).astype(BF16)
    length, patch_count = low.shape[0], placed.shape[2]
    slots = lax.broadcasted_iota(jnp.int32, (length, patch_count), 0)
    select = jnp.where(placed[0] == slots, 1.0, 0.0).astype(BF16)
    patch_grad[0] = dot(select, low, 0, 0)

    @pl.when(clip == 0)
    def _():
        norm_grad[...] = jnp.zeros_like(norm_grad)

    norm_grad[0:1] += gain_grad
    norm_grad[1:2] += shift_grad


def bits_of(count):
    return count.bit_length() - 1


def swap_pairs(index, bits):
    out = index & 1
    bit = 1
    while bit < bits:
        if bit + 1 < bits:
            out = out | ((index >> bit & 1) << (bit + 1)) | ((index >> (bit + 1) & 1) << bit)
            bit += 2
        else:
            out = out | (index >> bit & 1) << bit
            bit += 1
    return out


def partner(clip, mask, bits):
    return clip ^ (swap_pairs(mask, bits) if clip & 1 else mask)


def exchange(array, mask, bits, clips, shards):
    pairs = [
        (clip * shards + shard, partner(clip, mask, bits) * shards + shard)
        for clip in range(clips)
        for shard in range(shards)
    ]
    return lax.ppermute(array, ("clip", "tp"), pairs)


def shift(array, step, clips, shards):
    pairs = [
        (clip * shards + (shard + step) % shards, clip * shards + shard)
        for clip in range(clips)
        for shard in range(shards)
    ]
    return lax.ppermute(array, ("clip", "tp"), pairs)


def gather_shard(piece, clips, shards):
    bits = bits_of(GROUP)
    pair = jnp.stack([piece, exchange(piece, 2, bits, clips, shards)])
    near = jnp.concatenate([pair, exchange(pair, 4, bits, clips, shards)])
    return near, exchange(near, 1, bits, clips, shards)


def gather_order(clip_index):
    bits = bits_of(GROUP)
    me = clip_index % GROUP
    odd = me & 1

    def place(base, parity, code):
        return base ^ jnp.where(parity == 1, swap_pairs(code, bits), code)

    codes = (0, 2, 4, 6)
    near = [place(me, odd, code) for code in codes]
    far = [place(me ^ 1, 1 - odd, code) for code in codes]
    return near + far


def scatter_sum(stack, clips, shards):
    bits = bits_of(clips)
    if clips == 1:
        return stack[0]
    got = exchange(stack[1::2], 1, bits, clips, shards)
    keep = stack[0::2]
    turned = [swap_pairs(2 * j, bits) // 2 for j in range(clips // 2)]
    stack = jnp.stack([keep[j] + got[turned[j]] for j in range(clips // 2)])
    for bit in reversed(range(1, bits)):
        half = stack.shape[0] // 2
        got = exchange(stack[half:], 1 << bit, bits, clips, shards)
        stack = stack[:half] + got
    return stack[0]


def spread(piece, clips, shards):
    bits = bits_of(clips)
    stack = piece[None]
    for bit in range(1, bits):
        stack = jnp.concatenate([stack, exchange(stack, 1 << bit, bits, clips, shards)])
    if clips == 1:
        return [stack[0]]
    got = exchange(stack, 1, bits, clips, shards)
    out = []
    for q in range(clips):
        if q & 1:
            out.append(got[swap_pairs(q ^ 1, bits) // 2])
        else:
            out.append(stack[q // 2])
    return out


def clip_order(clip_index, clips):
    bits = bits_of(clips)
    return [
        clip_index ^ jnp.where(clip_index & 1 == 1, swap_pairs(q, bits), q) for q in range(clips)
    ]


def sum_all(array, clips, shards):
    for bit in range(bits_of(clips)):
        pairs = [
            (clip * shards + shard, (clip ^ 1 << bit) * shards + shard)
            for clip in range(clips)
            for shard in range(shards)
        ]
        array = array + lax.ppermute(array, ("clip", "tp"), pairs)
    return array


def own_part(array, axis_dim, clip_index, parts):
    part_width = array.shape[axis_dim] // parts
    return lax.dynamic_slice_in_dim(array, clip_index * part_width, part_width, axis_dim)


def adam_step(weight, gradient, first_mom, second_mom, rate):
    first_new = 0.5 * first_mom + 0.5 * gradient
    second_new = 0.5 * second_mom + 0.5 * gradient * gradient
    fix = 1.0 - 0.5**STEP
    direction = first_new / fix / (jnp.sqrt(second_new / fix) + 1e-08)
    return (weight - rate * (direction + 0.01 * weight), first_new, second_new)


def on_device(
    patches,
    keep_freq,
    keep_time,
    cotangent,
    w_qkv,
    w_out,
    w_up,
    w_down,
    norms,
    m_qkv,
    v_qkv,
    m_out,
    v_out,
    m_up,
    v_up,
    m_down,
    v_down,
    m_norms,
    v_norms,
):
    clip_count, length, width = cotangent.shape
    patch_count = patches.shape[1]
    clips, shards = lax.axis_size("clip"), lax.axis_size("tp")
    clip_index, shard_index = lax.axis_index("clip"), lax.axis_index("tp")
    local = w_qkv.shape[2]
    heads = local // HD
    hidden = w_up.shape[1]
    packed_width = 3 * local
    member = clip_index % GROUP

    qkv_rows = jnp.transpose(w_qkv, (1, 2, 0)).reshape(packed_width, width)

    def piece_of(rows):
        return own_part(rows, 0, member, GROUP)

    qkv_piece = piece_of(qkv_rows)
    rest_piece = jnp.concatenate([piece_of(w_out), piece_of(w_up), piece_of(w_down)])
    qkv_pieces = [
        gather_shard(shift(qkv_piece, step, clips, shards), clips, shards)
        for step in range(1, shards)
    ]
    rest_pieces = [
        gather_shard(shift(rest_piece, step, clips, shards), clips, shards)
        for step in range(1, shards)
    ]
    order = jnp.stack([*gather_order(clip_index), shard_index & 1]).astype(jnp.int32)

    placed, kept = positions(keep_freq, keep_time)
    placed = placed[:, None, :].astype(jnp.int32)
    kept = kept.astype(jnp.int32)

    row = functools.partial(clip_block, length)
    shape = jax.ShapeDtypeStruct
    rows_f32 = shape((clip_count, length, width), F32)
    rows_low = shape((clip_count, length, width), BF16)
    grid = (clip_count,)

    inputs, first, grad = call(
        front_kernel,
        grid,
        [clip_block(1, patch_count), clip_block(patch_count, width), row(width), whole_block(4, width)],
        [row(width)] * 3,
        [rows_f32, rows_low, rows_low],
        cost=(2 * clip_count * length * patch_count * width, 20_000_000),
    )(kept, order, placed, patches, cotangent, norms)

    packs, mixes, totals, qkv_lows = [], [], [], []
    for shard in range(shards):
        own = shard == 0
        packed, mixed, total, low = call(
            functools.partial(attend_kernel, own, heads),
            grid,
            [row(width)] + ([whole_block(packed_width, width)] if own else [ANY, ANY]),
            [
                clip_block(packed_width, length),
                clip_block(local, length),
                clip_block(heads, length),
                whole_block(packed_width, width),
            ],
            [
                shape((clip_count, packed_width, length), BF16),
                shape((clip_count, local, length), BF16),
                shape((clip_count, heads, length), F32),
                shape((packed_width, width), BF16),
            ],
            scratch=()
            if own
            else (pltpu.VMEM((packed_width, width), F32), pltpu.SemaphoreType.DMA((GROUP,))),
            cost=(6_000_000_000, 10_000_000),
        )(kept, order, first, *((qkv_rows,) if own else qkv_pieces[shard - 1]))
        packs.append(packed)
        mixes.append(mixed)
        totals.append(total)
        qkv_lows.append(low)

    middle, second, out_lows = call(
        functools.partial(project_kernel, shards),
        grid,
        [row(width), whole_block(4, width), whole_block(local, width)]
        + [ANY] * (2 * (shards - 1))
        + [clip_block(local, length)] * shards,
        [row(width), row(width), whole_block(shards, local, width)],
        [rows_f32, rows_low, shape((shards, local, width), BF16)],
        scratch=(
            pltpu.VMEM((shards - 1, local, width), F32),
            pltpu.SemaphoreType.DMA((shards - 1, GROUP)),
        ),
        cost=(2_000_000_000, 15_000_000),
    )(
        kept,
        order,
        inputs,
        norms,
        w_out,
        *[piece for pair in rest_pieces for piece in pair],
        *mixes,
    )

    branches, backs = [], []
    for shard in range(shards):
        own = shard == 0
        weights = shape((width, hidden), F32)
        results = call(
            functools.partial(mlp_kernel, own, 256),
            grid,
            [row(width), row(width)]
            + ([whole_block(width, hidden), whole_block(hidden, width)] if own else [ANY, ANY]),
            [row(width), row(width)] + ([whole_block(width, hidden)] * 2 if own else []),
            [rows_f32, rows_f32] + ([weights, weights] if own else []),
            scratch=(pltpu.VMEM((width, hidden), BF16), pltpu.VMEM((hidden, width), BF16))
            + (
                ()
                if own
                else (
                    pltpu.VMEM((2, width, hidden), F32),
                    pltpu.SemaphoreType.DMA((2, GROUP)),
                )
            ),
            cost=(8_000_000_000, 18_000_000),
        )(kept, order, second, grad, *((w_up, w_down) if own else rest_pieces[shard - 1]))
        branches.append(results[0])
        backs.append(results[1])
        if own:
            grad_up, grad_down = results[2:]

    block_out, grad_middle, middle_low, norm_grad2 = call(
        functools.partial(close_kernel, shards),
        grid,
        [row(width), row(width), whole_block(4, width)] + [row(width)] * (2 * shards),
        [row(width), row(width), row(width), whole_block(2, width)],
        [rows_low, rows_f32, rows_low, shape((2, width), F32)],
        cost=(100_000_000, 50_000_000),
    )(kept, order, middle, grad, norms, *branches, *backs)

    grad_packs = []
    for shard in range(shards):
        own = shard == 0
        results = call(
            functools.partial(attend_back_kernel, own, heads),
            grid,
            [
                clip_block(packed_width, length),
                clip_block(local, length),
                clip_block(heads, length),
                row(width),
                pl.BlockSpec((1, local, width), functools.partial(lambda s, *_: (s, 0, 0), shard)),
            ]
            + ([row(width)] if own else []),
            [clip_block(packed_width, length)]
            + ([whole_block(width, packed_width), whole_block(width, local)] if own else []),
            [shape((clip_count, packed_width, length), BF16)]
            + (
                [shape((width, packed_width), F32), shape((width, local), F32)] if own else []
            ),
            cost=(10_000_000_000, 10_000_000),
        )(
            kept,
            order,
            packs[shard],
            mixes[shard],
            totals[shard],
            middle_low,
            out_lows,
            *((first,) if own else ()),
        )
        grad_packs.append(results[0])
        if own:
            grad_qkv, grad_out = results[1:]

    patch_grad, norm_grad1 = call(
        functools.partial(final_kernel, shards),
        grid,
        [clip_block(1, patch_count), row(width), row(width), whole_block(4, width)]
        + [clip_block(packed_width, length)] * shards
        + [whole_block(packed_width, width)] * shards,
        [clip_block(patch_count, width), whole_block(2, width)],
        [shape((clip_count, patch_count, width), F32), shape((2, width), F32)],
        cost=(8_000_000_000, 30_000_000),
    )(kept, order, placed, inputs, grad_middle, norms, *grad_packs, *qkv_lows)

    places = clip_order(clip_index, clips)
    part = width // clips

    def to_stack(array):
        blocks = array.reshape(clips, part, array.shape[1])
        return jnp.concatenate([lax.dynamic_slice_in_dim(blocks, at, 1, 0) for at in places])

    def from_list(pieces):
        stack = jnp.stack(pieces)
        bits = bits_of(clips)
        order_back = []
        for piece in range(clips):
            code = piece ^ clip_index
            order_back.append(jnp.where(clip_index & 1 == 1, swap_pairs(code, bits), code))
        return jnp.concatenate(
            [lax.dynamic_slice_in_dim(stack, at, 1, 0) for at in order_back]
        ).reshape(clips * part, -1)

    rate_model = D ** (-0.5)
    rest_sum = scatter_sum(
        to_stack(jnp.concatenate([grad_out, grad_up, grad_down], axis=1)), clips, shards
    )
    qkv_sum = scatter_sum(to_stack(grad_qkv), clips, shards)
    out_new = adam_step(
        own_part(w_out, 1, clip_index, clips),
        rest_sum[:, :local].T,
        m_out,
        v_out,
        max(16 * D // BLOCK, 1) ** (-0.5),
    )
    up_new = adam_step(
        own_part(w_up, 0, clip_index, clips), rest_sum[:, local : local + hidden], m_up, v_up, rate_model
    )
    down_new = adam_step(
        own_part(w_down, 1, clip_index, clips),
        rest_sum[:, local + hidden :].T,
        m_down,
        v_down,
        FF ** (-0.5),
    )
    qkv_new = adam_step(
        own_part(w_qkv, 0, clip_index, clips),
        qkv_sum.reshape(part, 3, local),
        m_qkv,
        v_qkv,
        rate_model,
    )
    rest_full = from_list(
        spread(jnp.concatenate([out_new[0].T, up_new[0], down_new[0].T], axis=1), clips, shards)
    )
    qkv_full = from_list(spread(qkv_new[0].reshape(part, packed_width), clips, shards))
    full_out = rest_full[:, :local].T
    full_up = rest_full[:, local : local + hidden]
    full_down = rest_full[:, local + hidden :].T
    full_qkv = qkv_full.reshape(width, 3, local)

    norm_sum = sum_all(jnp.concatenate([norm_grad1, norm_grad2]), clips, shards)
    piece_norms = own_part(norm_sum, 1, clip_index, clips)
    norms_new = adam_step(own_part(norms, 1, clip_index, clips), piece_norms, m_norms, v_norms, 0.3)
    full_norms = lax.all_gather(norms_new[0], "clip", axis=1, tiled=True)

    return (
        block_out,
        patch_grad,
        piece_norms,
        full_qkv,
        full_out,
        full_up,
        full_down,
        full_norms,
        qkv_new[1],
        out_new[1],
        up_new[1],
        down_new[1],
        norms_new[1],
        qkv_new[2],
        out_new[2],
        up_new[2],
        down_new[2],
        norms_new[2],
        full_qkv.astype(BF16),
        full_out.astype(BF16),
        full_up.astype(BF16),
        full_down.astype(BF16),
    )


def solution(mesh):
    return jax.shard_map(
        on_device,
        mesh=mesh,
        in_specs=(
            P("clip", None, None),
            P("clip", None),
            P("clip", None),
            P("clip", None, None),
            P(None, None, "tp"),
            P("tp", None),
            P(None, "tp"),
            P("tp", None),
            P(),
            P("clip", None, "tp"),
            P("clip", None, "tp"),
            P("tp", "clip"),
            P("tp", "clip"),
            P("clip", "tp"),
            P("clip", "tp"),
            P("tp", "clip"),
            P("tp", "clip"),
            P(None, "clip"),
            P(None, "clip"),
        ),
        out_specs=(
            P("clip", None, None),
            P("clip", None, None),
            P(None, "clip"),
            P(None, None, "tp"),
            P("tp", None),
            P(None, "tp"),
            P("tp", None),
            P(),
            P("clip", None, "tp"),
            P("tp", "clip"),
            P("clip", "tp"),
            P("tp", "clip"),
            P(None, "clip"),
            P("clip", None, "tp"),
            P("tp", "clip"),
            P("clip", "tp"),
            P("tp", "clip"),
            P(None, "clip"),
            P(None, None, "tp"),
            P("tp", None),
            P(None, "tp"),
            P("tp", None),
        ),
        check_vma=False,
    )
```

time: 1050 us -> 544 us (0.52)
  waiting for transfers between devices: 773 us -> 101 us
  Pallas kernels: 0 us -> 223 us
  matrix products: 81.6 us -> 0 us
  local copies, waits for them, and re-layouts: 59.3 us -> 116 us
  blocking collectives: 44.5 us -> 9.14 us
  starting transfers between devices: 1.12 us -> 36.3 us
  other arithmetic: 75.4 us -> 50.9 us
  between operations: 14.9 us -> 1.94 us
    psum x4 -> x0, waiting for transfers between devices: 721 us -> none  [the longest x1 297 us: on_device(): lax.psum(jnp.dot(active_low, down_low, preferred_element_type=jnp.float32...]
    pallas_call x0 -> x16, Pallas kernels: none -> 223 us  [the longest x4 62.3 us: on_device(): call(functools.partial(mlp_kernel, own, 256), grid, [row(width), row(widt...]
    ppermute x0 -> x39, waiting for transfers between devices: none -> 101 us  [the longest x6 60.3 us: shift(): return lax.ppermute(array, ('clip', 'tp'), pairs)]
    dot_general x27 -> x0, matrix products: 78.8 us -> none  [the longest x1 11.7 us: on_device(): hidden = jnp.dot(second_low, up_low, preferred_element_type=jnp.float32)]
    unnamed x86 -> x179, local copies, waits for them, and re-layouts: 27.8 us -> 79.5 us
    all_gather x3 -> x0, waiting for transfers between devices: 51.6 us -> none  [the longest x1 28.1 us: on_device(): lax.all_gather(up_new[0], 'clip', axis=0, tiled=True)]
    ppermute x0 -> x39, starting transfers between devices: none -> 36.3 us  [the longest x30 26.8 us: exchange(): return lax.ppermute(array, ('clip', 'tp'), pairs)]
    reduce_sum x11 -> x0, other arithmetic: 29.6 us -> none  [the longest x3 11.1 us: layer_norm(): centre = values - jnp.mean(values, axis=-1, keepdims=True)]
  transfers between devices with their start and end apart: 7 -> 39, of which waited for: 6 -> 10; matrix products, arithmetic and copies ran while one was open for 5% -> 24% of each run, Pallas kernels for 0% -> 21%
where the time goes in v1:
time: 544 us; the launch traced here: 538 us
  Pallas kernels  223 us (41%)
  local copies, waits for them, and re-layouts  116 us (21%)
  waiting for transfers between devices  101 us (19%)
  other arithmetic  50.9 us (9%)
  starting transfers between devices  36.3 us (7%)
  blocking collectives  9.14 us (2%)
    unnamed x179, local copies, waits for them, and re-layouts  79.5 us
    pallas_call x4, Pallas kernels, on_device(): call(functools.partial(mlp_kernel, own, 256), grid, [row(width), row(widt...  62.3 us
    ppermute x6, waiting for transfers between devices, shift(): return lax.ppermute(array, ('clip', 'tp'), pairs)  60.3 us
    pallas_call x4, Pallas kernels, on_device(): call(functools.partial(attend_back_kernel, own, heads), grid, [clip_block...  55.1 us
    pallas_call x4, Pallas kernels, on_device(): call(functools.partial(attend_kernel, own, heads), grid, [row(width)] + (...  45.6 us
    ppermute x30, waiting for transfers between devices, exchange(): return lax.ppermute(array, ('clip', 'tp'), pairs)  39.4 us
    ppermute x30, starting transfers between devices, exchange(): return lax.ppermute(array, ('clip', 'tp'), pairs)  26.8 us
    pallas_call x1, Pallas kernels, on_device(): call(functools.partial(final_kernel, shards), grid, [clip_block(1, patch_...  22.2 us
  transfers between devices with their start and end apart: 39, of which 10 were waited for; matrix products, arithmetic and copies ran while one was open for 24% of the time, Pallas kernels for 21%

profile of v1, /device:TPU:0, one launch (start us, length us, event | category | flops | bytes accessed | tf_op | source)
XLA Modules:
  0.0 537.9 jit_solution(16983559126248110637)
XLA Ops:
  2.7 3.1 collective-permute-start.8
  8.8 14.8 %collective-permute-done.8 = f32[216,768]{1,0:T(8,128)S(1)} collective-permute-done((f32[216,768]{1,0:T(8,128)S(1)}, f32[216,768]{1,0:T(8,128)S(1)}, u32[]{:S(2)}, u32[]{:S(2)}) %collective-permute-start.8) | collective-permute-done | bytes 663584 | tf_op jit(solution)/shard_map/ppermute | solution.py:401
  25.4 11.0 %collective-permute-done = f32[216,768]{1,0:T(8,128)S(1)} collective-permute-done((f32[216,768]{1,0:T(8,128)S(1)}, f32[216,768]{1,0:T(8,128)S(1)}, u32[]{:S(2)}, u32[]{:S(2)}) %collective-permute-start) | collective-permute-done | bytes 663584 | tf_op jit(solution)/shard_map/ppermute | solution.py:401
  37.9 27.5 %collective-permute-done.4 = f32[216,768]{1,0:T(8,128)S(1)} collective-permute-done((f32[216,768]{1,0:T(8,128)S(1)}, f32[216,768]{1,0:T(8,128)S(1)}, u32[]{:S(2)}, u32[]{:S(2)}) %collective-permute-start.4) | collective-permute-done | bytes 663584 | tf_op jit(solution)/shard_map/ppermute | solution.py:401
  81.0 7.0 %collective-permute-done.16 = f32[72,768]{1,0:T(8,128)} collective-permute-done((f32[72,768]{1,0:T(8,128)}, f32[72,768]{1,0:T(8,128)}, u32[]{:S(2)}, u32[]{:S(2)}) %collective-permute-start.16) | collective-permute-done | bytes 221216 | tf_op jit(solution)/shard_map/ppermute | solution.py:401
  90.1 6.4 %collective-permute-done.13 = f32[72,768]{1,0:T(8,128)S(1)} collective-permute-done((f32[72,768]{1,0:T(8,128)}, f32[72,768]{1,0:T(8,128)S(1)}, u32[]{:S(2)}, u32[]{:S(2)}) %collective-permute-start.13) | collective-permute-done | bytes 221216 | tf_op jit(solution)/shard_map/ppermute | solution.py:392
  103.4 4.3 copy.81.patches
  110.6 21.0 %collective-permute-done.14 = f32[2,72,768]{2,1,0:T(8,128)S(1)} collective-permute-done((f32[2,72,768]{2,1,0:T(8,128)S(1)}, f32[2,72,768]{2,1,0:T(8,128)S(1)}, u32[]{:S(2)}, u32[]{:S(2)}) %collective-permute-start.14) | collective-permute-done | bytes 442400 | tf_op jit(solution)/shard_map/ppermute | solution.py:392
  137.6 3.8 pad_maximum_fusion.1.refs_3_.refs_0_
  141.8 3.0 pad_maximum_fusion.2.refs_5_.refs_0_
  144.9 9.1 %shard_map.354 = (f32[2,704,768]{2,1,0:T(8,128)}, bf16[2,704,768]{2,1,0:T(8,128)(2,1)}, bf16[2,704,768]{2,1,0:T(8,128)(2,1)}) custom-call(s32[2]{0:T(128)} %mul.176.kept, s32[9]{0:T(128)} %stack.117.order, s32[2,1,1188]{2,1,0:T(1,128)} %select_n.209.placed.refs_0_, bf16[2,1188,768]{2,1,0:T(8,128)(2,1)} %copy.81.patches, bf16[2,704,768]{2,1,0:T(8,128)(2,1)} %cot.1, ...), custom_call_target="tpu_custom_call" | custom-call | flops 2569273344 | bytes 20000000 | tf_op jit(solution)/shard_map/pallas_call | solution.py:546
  156.7 10.6 %shard_map.355 = (bf16[2,576,704]{2,1,0:T(8,128)(2,1)}, bf16[2,192,704]{2,1,0:T(8,128)(2,1)}, f32[2,3,704]{2,1,0:T(4,128)}, bf16[576,768]{1,0:T(8,128)(2,1)}) custom-call(s32[2]{0:T(128)} %mul.176.kept, s32[9]{0:T(128)} %stack.117.order, bf16[2,704,768]{2,1,0:T(8,128)(2,1)} %get-tuple-element.64.first.refs_0_, f32[576,768]{1,0:T(8,128)} %bitcast.105), custom_call_target="tpu_custom_call" | custom-call | flops 6000000000 | bytes 10000000 | tf_op jit(solution)/shard_map/pallas_call | solution.py:558
  168.0 11.5 %shard_map.356 = (bf16[2,576,704]{2,1,0:T(8,128)(2,1)}, bf16[2,192,704]{2,1,0:T(8,128)(2,1)}, f32[2,3,704]{2,1,0:T(4,128)}, bf16[576,768]{1,0:T(8,128)(2,1)}) custom-call(s32[2]{0:T(128)} %mul.176.kept, s32[9]{0:T(128)} %stack.117.order, bf16[2,704,768]{2,1,0:T(8,128)(2,1)} %get-tuple-element.64.first.refs_0_, f32[4,72,768]{2,1,0:T(8,128)} %pad_maximum_fusion.10.refs_0_, ...), custom_call_target="tpu_custom_call" | custom-call | flops 6000000000 | bytes 10000000 | tf_op jit(solution)/shard_map/pallas_call | solution.py:558
  179.5 11.5 %shard_map.357 = (bf16[2,576,704]{2,1,0:T(8,128)(2,1)}, bf16[2,192,704]{2,1,0:T(8,128)(2,1)}, f32[2,3,704]{2,1,0:T(4,128)}, bf16[576,768]{1,0:T(8,128)(2,1)}) custom-call(s32[2]{0:T(128)} %mul.176.kept, s32[9]{0:T(128)} %stack.117.order, bf16[2,704,768]{2,1,0:T(8,128)(2,1)} %get-tuple-element.64.first.refs_0_, f32[4,72,768]{2,1,0:T(8,128)} %pad_maximum_fusion.11.refs_0_, ...), custom_call_target="tpu_custom_call" | custom-call | flops 6000000000 | bytes 10000000 | tf_op jit(solution)/shard_map/pallas_call | solution.py:558
  191.9 12.0 %shard_map.358 = (bf16[2,576,704]{2,1,0:T(8,128)(2,1)}, bf16[2,192,704]{2,1,0:T(8,128)(2,1)}, f32[2,3,704]{2,1,0:T(4,128)}, bf16[576,768]{1,0:T(8,128)(2,1)}) custom-call(s32[2]{0:T(128)} %mul.176.kept, s32[9]{0:T(128)} %stack.117.order, bf16[2,704,768]{2,1,0:T(8,128)(2,1)} %get-tuple-element.64.first.refs_0_, f32[4,72,768]{2,1,0:T(8,128)} %copy-done.35, ...), custom_call_target="tpu_custom_call" | custom-call | flops 6000000000 | bytes 10000000 | tf_op jit(solution)/shard_map/pallas_call | solution.py:558
  203.9 10.1 %shard_map.359 = (f32[2,704,768]{2,1,0:T(8,128)}, bf16[2,704,768]{2,1,0:T(8,128)(2,1)}, bf16[4,192,768]{2,1,0:T(8,128)(2,1)}) custom-call(s32[2]{0:T(128)} %mul.176.kept, s32[9]{0:T(128)} %stack.117.order, f32[2,704,768]{2,1,0:T(8,128)} %get-tuple-element.63.refs_0_.refs_1_, f32[4,768]{1,0:T(4,128)} %refs_3_.1, f32[192,768]{1,0:T(8,128)} %refs_2_.2, ...), custom_call_target="tpu_custom_call" | custom-call | flops 2000000000 | bytes 15000000 | tf_op jit(solution)/shard_map/pallas_call | solution.py:584
  214.0 18.6 %shard_map.360 = (f32[2,704,768]{2,1,0:T(8,128)}, f32[2,704,768]{2,1,0:T(8,128)}, f32[768,768]{1,0:T(8,128)}, f32[768,768]{1,0:T(8,128)}) custom-call(s32[2]{0:T(128)} %mul.176.kept, s32[9]{0:T(128)} %stack.117.order, bf16[2,704,768]{2,1,0:T(8,128)(2,1)} %get-tuple-element.71.second, bf16[2,704,768]{2,1,0:T(8,128)(2,1)} %get-tuple-element.70.grad.refs_1_, ...), custom_call_target="tpu_custom_call" | custom-call | flops 8000000000 | bytes 18000000 | tf_op jit(solution)/shard_map/pallas_call | solution.py:611
  232.6 14.7 %shard_map.363 = (f32[2,704,768]{2,1,0:T(8,128)}, f32[2,704,768]{2,1,0:T(8,128)}) custom-call(s32[2]{0:T(128)} %mul.176.kept, s32[9]{0:T(128)} %stack.117.order, bf16[2,704,768]{2,1,0:T(8,128)(2,1)} %get-tuple-element.71.second, bf16[2,704,768]{2,1,0:T(8,128)(2,1)} %get-tuple-element.70.grad.refs_1_, f32[4,216,768]{2,1,0:T(8,128)} %copy-done.1, ...), custom_call_target="tpu_custom_call" | custom-call | flops 8000000000 | bytes 18000000 | tf_op jit(solution)/shard_map/pallas_call | solution.py:611
  247.4 14.5 %shard_map.362 = (f32[2,704,768]{2,1,0:T(8,128)}, f32[2,704,768]{2,1,0:T(8,128)}) custom-call(s32[2]{0:T(128)} %mul.176.kept, s32[9]{0:T(128)} %stack.117.order, bf16[2,704,768]{2,1,0:T(8,128)(2,1)} %get-tuple-element.71.second, bf16[2,704,768]{2,1,0:T(8,128)(2,1)} %get-tuple-element.70.grad.refs_1_, f32[4,216,768]{2,1,0:T(8,128)} %pad_maximum_fusion.2.refs_5_.refs_0_, ...), custom_call_target="tpu_custom_call" | custom-call | flops 8000000000 | bytes 18000000 | tf_op jit(solution)/shard_map/pallas_call | solution.py:611
  261.8 14.5 %shard_map.361 = (f32[2,704,768]{2,1,0:T(8,128)}, f32[2,704,768]{2,1,0:T(8,128)}) custom-call(s32[2]{0:T(128)} %mul.176.kept, s32[9]{0:T(128)} %stack.117.order, bf16[2,704,768]{2,1,0:T(8,128)(2,1)} %get-tuple-element.71.second, bf16[2,704,768]{2,1,0:T(8,128)(2,1)} %get-tuple-element.70.grad.refs_1_, f32[4,216,768]{2,1,0:T(8,128)} %pad_maximum_fusion.1.refs_3_.refs_0_, ...), custom_call_target="tpu_custom_call" | custom-call | flops 8000000000 | bytes 18000000 | tf_op jit(solution)/shard_map/pallas_call | solution.py:611
  276.3 18.3 %shard_map.364 = (bf16[2,704,768]{2,1,0:T(8,128)(2,1)}, f32[2,704,768]{2,1,0:T(8,128)}, bf16[2,704,768]{2,1,0:T(8,128)(2,1)}, f32[2,768]{1,0:T(2,128)}) custom-call(s32[2]{0:T(128)} %mul.176.kept, s32[9]{0:T(128)} %stack.117.order, f32[2,704,768]{2,1,0:T(8,128)} %get-tuple-element.69.refs_0_, bf16[2,704,768]{2,1,0:T(8,128)(2,1)} %get-tuple-element.70.grad.refs_1_, ...), custom_call_target="tpu_custom_call" | custom-call | flops 100000000 | bytes 50000000 | tf_op jit(solution)/shard_map/pallas_call | solution.py:634
  294.6 17.1 %shard_map.365 = (bf16[2,576,704]{2,1,0:T(8,128)(2,1)}, f32[768,576]{1,0:T(8,128)}, f32[768,192]{1,0:T(8,128)}) custom-call(s32[2]{0:T(128)} %mul.176.kept, s32[9]{0:T(128)} %stack.117.order, bf16[2,576,704]{2,1,0:T(8,128)(2,1)} %get-tuple-element.82.packed, bf16[2,192,704]{2,1,0:T(8,128)(2,1)} %get-tuple-element.65.refs_9_.mixed, ...), custom_call_target="tpu_custom_call" | custom-call | flops 10000000000 | bytes 10000000 | tf_op jit(solution)/shard_map/pallas_call | solution.py:646
  311.8 6.7 %concatenate.78 = f32[768,1728]{1,0:T(8,128)} concatenate(f32[768,192]{1,0:T(8,128)} %get-tuple-element.101, f32[768,768]{1,0:T(8,128)S(1)} %copy-done.17, f32[768,768]{1,0:T(8,128)} %get-tuple-element.103), dimensions={1} | concatenate | bytes 10616832 | tf_op jit(solution)/shard_map/concatenate | solution.py:709
  361.4 2.9 slice_add_fusion.4
  368.0 12.6 %shard_map.368.refs_7_ = bf16[2,576,704]{2,1,0:T(8,128)(2,1)} custom-call(s32[2]{0:T(128)} %mul.176.kept, s32[9]{0:T(128)} %stack.117.order, bf16[2,576,704]{2,1,0:T(8,128)(2,1)} %get-tuple-element.91.packed, bf16[2,192,704]{2,1,0:T(8,128)(2,1)} %get-tuple-element.68.refs_12_.mixed, f32[2,3,704]{2,1,0:T(4,128)} %get-tuple-element.92.total, ...), custom_call_target="tpu_custom_call" | custom-call | flops 10000000000 | bytes 10000000 | tf_op jit(solution)/shard_map/pallas_call | solution.py:646
  380.6 8.8 %collective-permute-done.28 = f32[2,96,576]{2,1,0:T(8,128)} collective-permute-done((f32[2,96,576]{2,1,0:T(8,128)S(1)}, f32[2,96,576]{2,1,0:T(8,128)}, u32[]{:S(2)}, u32[]{:S(2)}) %collective-permute-start.28) | collective-permute-done | bytes 442400 | tf_op jit(solution)/shard_map/ppermute | solution.py:392
  394.4 12.9 %shard_map.367.refs_6_ = bf16[2,576,704]{2,1,0:T(8,128)(2,1)} custom-call(s32[2]{0:T(128)} %mul.176.kept, s32[9]{0:T(128)} %stack.117.order, bf16[2,576,704]{2,1,0:T(8,128)(2,1)} %get-tuple-element.89.packed, bf16[2,192,704]{2,1,0:T(8,128)(2,1)} %get-tuple-element.67.refs_11_.mixed, f32[2,3,704]{2,1,0:T(4,128)} %get-tuple-element.90.total, ...), custom_call_target="tpu_custom_call" | custom-call | flops 10000000000 | bytes 10000000 | tf_op jit(solution)/shard_map/pallas_call | solution.py:646
  415.5 12.5 %shard_map.366.refs_5_ = bf16[2,576,704]{2,1,0:T(8,128)(2,1)} custom-call(s32[2]{0:T(128)} %mul.176.kept, s32[9]{0:T(128)} %stack.117.order, bf16[2,576,704]{2,1,0:T(8,128)(2,1)} %get-tuple-element.87.packed, bf16[2,192,704]{2,1,0:T(8,128)(2,1)} %get-tuple-element.66.refs_10_.mixed, f32[2,3,704]{2,1,0:T(4,128)} %get-tuple-element.88.total, ...), custom_call_target="tpu_custom_call" | custom-call | flops 10000000000 | bytes 10000000 | tf_op jit(solution)/shard_map/pallas_call | solution.py:646
  432.4 22.2 %shard_map.369 = (f32[2,1188,768]{2,1,0:T(8,128)}, f32[2,768]{1,0:T(2,128)}) custom-call(s32[2]{0:T(128)} %mul.176.kept, s32[9]{0:T(128)} %stack.117.order, s32[2,1,1188]{2,1,0:T(1,128)} %select_n.209.placed.refs_0_, f32[2,704,768]{2,1,0:T(8,128)} %get-tuple-element.63.refs_0_.refs_1_, f32[2,704,768]{2,1,0:T(8,128)} %get-tuple-element.81.refs_2_, ...), custom_call_target="tpu_custom_call" | custom-call | flops 8000000000 | bytes 30000000 | tf_op jit(solution)/shard_map/pallas_call | solution.py:678
  457.8 15.5 %copy.117 = f32[2,1188,768]{2,0,1:T(2,128)} copy(f32[2,1188,768]{2,1,0:T(8,128)} %get-tuple-element.149) | data formatting | bytes 14598144
  480.5 9.1 %all-gather = f32[8,96,4]{1,2,0:T(4,128)S(1)} all-gather(f32[1,96,4]{1,2,0:T(4,128)S(1)} %get-tuple-element.172), channel_id=1, replica_groups=mesh['clip'=8,'tp'=4] {'clip'}, dimensions={0}, use_global_device_ids=true | all-gather | bytes 13824 | tf_op jit(solution)/shard_map/all_gather | solution.py:748
  527.5 3.8 fusion.8
  (318 shorter events, 164.5 us)
Async XLA Ops:
  2.7 20.9 %collective-permute-start.8 = (f32[216,768]{1,0:T(8,128)S(1)}, f32[216,768]{1,0:T(8,128)S(1)}, u32[]{:S(2)}, u32[]{:S(2)}) collective-permute-start(f32[216,768]{1,0:T(8,128)S(1)} %pad_maximum_fusion.13), channel_id=1, source_target_pairs={{3,0},{0,1},{1,2},{2,3},{7,4},{4,5},{5,6},{6,7},{11,8},{8,9},{9,10... | collective-permute-start | bytes 1990664 | tf_op jit(solution)/shard_map/ppermute | solution.py:401
  5.8 30.6 %collective-permute-start = (f32[216,768]{1,0:T(8,128)S(1)}, f32[216,768]{1,0:T(8,128)S(1)}, u32[]{:S(2)}, u32[]{:S(2)}) collective-permute-start(f32[216,768]{1,0:T(8,128)S(1)} %pad_maximum_fusion.13), channel_id=1, source_target_pairs={{1,0},{2,1},{3,2},{0,3},{5,4},{6,5},{7,6},{4,7},{9,8},{10,9},{11,1... | collective-permute-start | bytes 1990664 | tf_op jit(solution)/shard_map/ppermute | solution.py:401
  7.9 57.5 %collective-permute-start.4 = (f32[216,768]{1,0:T(8,128)S(1)}, f32[216,768]{1,0:T(8,128)S(1)}, u32[]{:S(2)}, u32[]{:S(2)}) collective-permute-start(f32[216,768]{1,0:T(8,128)S(1)} %pad_maximum_fusion.13), channel_id=1, source_target_pairs={{2,0},{3,1},{0,2},{1,3},{6,4},{7,5},{4,6},{5,7},{10,8},{11,9},{8,1... | collective-permute-start | bytes 1990664 | tf_op jit(solution)/shard_map/ppermute | solution.py:401
  23.6 46.8 %collective-permute-start.9 = (f32[216,768]{1,0:T(8,128)S(1)}, f32[216,768]{1,0:T(8,128)}, u32[]{:S(2)}, u32[]{:S(2)}) collective-permute-start(f32[216,768]{1,0:T(8,128)S(1)} %collective-permute-done.8), channel_id=1, source_target_pairs={{0,8},{1,9},{2,10},{3,11},{4,20},{5,21},{6,22},{7,23},{8,0},{9,1},... | collective-permute-start | bytes 1990664 | tf_op jit(solution)/shard_map/ppermute | solution.py:392
  36.4 36.9 %collective-permute-start.1 = (f32[216,768]{1,0:T(8,128)S(1)}, f32[216,768]{1,0:T(8,128)S(1)}, u32[]{:S(2)}, u32[]{:S(2)}) collective-permute-start(f32[216,768]{1,0:T(8,128)S(1)} %collective-permute-done), channel_id=1, source_target_pairs={{0,8},{1,9},{2,10},{3,11},{4,20},{5,21},{6,22},{7,23},{8,0},{9,1},... | collective-permute-start | bytes 1990664 | tf_op jit(solution)/shard_map/ppermute | solution.py:392
  70.2 17.8 %collective-permute-start.16 = (f32[72,768]{1,0:T(8,128)}, f32[72,768]{1,0:T(8,128)}, u32[]{:S(2)}, u32[]{:S(2)}) collective-permute-start(f32[72,768]{1,0:T(8,128)} %constant_dynamic-slice_fusion.13), channel_id=1, source_target_pairs={{2,0},{3,1},{0,2},{1,3},{6,4},{7,5},{4,6},{5,7},{10,8},{11,9},{8,1... | collective-permute-start | bytes 663560 | tf_op jit(solution)/shard_map/ppermute | solution.py:401
  70.4 19.0 %collective-permute-start.20 = (f32[72,768]{1,0:T(8,128)}, f32[72,768]{1,0:T(8,128)S(1)}, u32[]{:S(2)}, u32[]{:S(2)}) collective-permute-start(f32[72,768]{1,0:T(8,128)} %constant_dynamic-slice_fusion.13), channel_id=1, source_target_pairs={{3,0},{0,1},{1,2},{2,3},{7,4},{4,5},{5,6},{6,7},{11,8},{8,9},{9,10... | collective-permute-start | bytes 663560 | tf_op jit(solution)/shard_map/ppermute | solution.py:401
  73.3 61.7 %collective-permute-start.10 = (f32[2,216,768]{2,1,0:T(8,128)}, f32[2,216,768]{2,1,0:T(8,128)}, u32[]{:S(2)}, u32[]{:S(2)}) collective-permute-start(f32[2,216,768]{2,1,0:T(8,128)} %pad_maximum_fusion.8), channel_id=1, source_target_pairs={{0,16},{1,17},{2,18},{3,19},{4,12},{5,13},{6,14},{7,15},{8,24},{9,... | collective-permute-start | bytes 3981320 | tf_op jit(solution)/shard_map/ppermute | solution.py:392
  76.9 60.2 %collective-permute-start.2 = (f32[2,216,768]{2,1,0:T(8,128)}, f32[2,216,768]{2,1,0:T(8,128)}, u32[]{:S(2)}, u32[]{:S(2)}) collective-permute-start(f32[2,216,768]{2,1,0:T(8,128)} %pad_maximum_fusion.6), channel_id=1, source_target_pairs={{0,16},{1,17},{2,18},{3,19},{4,12},{5,13},{6,14},{7,15},{8,24},{9,... | collective-permute-start | bytes 3981320 | tf_op jit(solution)/shard_map/ppermute | solution.py:392
  80.6 60.8 %collective-permute-start.6 = (f32[2,216,768]{2,1,0:T(8,128)}, f32[2,216,768]{2,1,0:T(8,128)}, u32[]{:S(2)}, u32[]{:S(2)}) collective-permute-start(f32[2,216,768]{2,1,0:T(8,128)} %pad_maximum_fusion.7), channel_id=1, source_target_pairs={{0,16},{1,17},{2,18},{3,19},{4,12},{5,13},{6,14},{7,15},{8,24},{9,... | collective-permute-start | bytes 3981320 | tf_op jit(solution)/shard_map/ppermute | solution.py:392
  96.5 12.7 %collective-permute-start.21 = (f32[72,768]{1,0:T(8,128)S(1)}, f32[72,768]{1,0:T(8,128)S(1)}, u32[]{:S(2)}, u32[]{:S(2)}) collective-permute-start(f32[72,768]{1,0:T(8,128)S(1)} %collective-permute-done.20), channel_id=1, source_target_pairs={{0,8},{1,9},{2,10},{3,11},{4,20},{5,21},{6,22},{7,23},{8,0},{9,1},... | collective-permute-start | bytes 663560 | tf_op jit(solution)/shard_map/ppermute | solution.py:392
  101.3 30.3 %collective-permute-start.14 = (f32[2,72,768]{2,1,0:T(8,128)S(1)}, f32[2,72,768]{2,1,0:T(8,128)S(1)}, u32[]{:S(2)}, u32[]{:S(2)}) collective-permute-start(f32[2,72,768]{2,1,0:T(8,128)S(1)} %pad_maximum_fusion.16), channel_id=1, source_target_pairs={{0,16},{1,17},{2,18},{3,19},{4,12},{5,13},{6,14},{7,15},{8,24},{9,... | collective-permute-start | bytes 1327112 | tf_op jit(solution)/shard_map/ppermute | solution.py:392
  109.3 35.5 %collective-permute-start.18 = (f32[2,72,768]{2,1,0:T(8,128)S(1)}, f32[2,72,768]{2,1,0:T(8,128)S(1)}, u32[]{:S(2)}, u32[]{:S(2)}) collective-permute-start(f32[2,72,768]{2,1,0:T(8,128)S(1)} %pad_maximum_fusion.17), channel_id=1, source_target_pairs={{0,16},{1,17},{2,18},{3,19},{4,12},{5,13},{6,14},{7,15},{8,24},{9,... | collective-permute-start | bytes 1327112 | tf_op jit(solution)/shard_map/ppermute | solution.py:392
  131.6 24.4 %collective-permute-start.22 = (f32[2,72,768]{2,1,0:T(8,128)S(1)}, f32[2,72,768]{2,1,0:T(8,128)S(1)}, u32[]{:S(2)}, u32[]{:S(2)}) collective-permute-start(f32[2,72,768]{2,1,0:T(8,128)S(1)} %pad_maximum_fusion.18), channel_id=1, source_target_pairs={{0,16},{1,17},{2,18},{3,19},{4,12},{5,13},{6,14},{7,15},{8,24},{9,... | collective-permute-start | bytes 1327112 | tf_op jit(solution)/shard_map/ppermute | solution.py:392
  135.1 32.4 %collective-permute-start.15 = (f32[4,72,768]{2,1,0:T(8,128)}, f32[4,72,768]{2,1,0:T(8,128)}, u32[]{:S(2)}, u32[]{:S(2)}) collective-permute-start(f32[4,72,768]{2,1,0:T(8,128)} %pad_maximum_fusion.10.refs_0_), channel_id=1, source_target_pairs={{0,4},{1,5},{2,6},{3,7},{4,0},{5,1},{6,2},{7,3},{8,12},{9,13},{10,... | collective-permute-start | bytes 2654216 | tf_op jit(solution)/shard_map/ppermute | solution.py:392
  137.1 66.8 %collective-permute-start.11 = (f32[4,216,768]{2,1,0:T(8,128)S(1)}, f32[4,216,768]{2,1,0:T(8,128)}, u32[]{:S(2)}, u32[]{:S(2)}) collective-permute-start(f32[4,216,768]{2,1,0:T(8,128)S(1)} %pad_maximum_fusion.3.refs_7_.refs_0_), channel_id=1, source_target_pairs={{0,4},{1,5},{2,6},{3,7},{4,0},{5,1},{6,2},{7,3},{8,12},{9,13},{10,... | collective-permute-start | bytes 7962632 | tf_op jit(solution)/shard_map/ppermute | solution.py:392
  141.4 62.5 %collective-permute-start.3 = (f32[4,216,768]{2,1,0:T(8,128)}, f32[4,216,768]{2,1,0:T(8,128)}, u32[]{:S(2)}, u32[]{:S(2)}) collective-permute-start(f32[4,216,768]{2,1,0:T(8,128)} %pad_maximum_fusion.1.refs_3_.refs_0_), channel_id=1, source_target_pairs={{0,4},{1,5},{2,6},{3,7},{4,0},{5,1},{6,2},{7,3},{8,12},{9,13},{10,... | collective-permute-start | bytes 7962632 | tf_op jit(solution)/shard_map/ppermute | solution.py:392
  144.8 59.1 %collective-permute-start.7 = (f32[4,216,768]{2,1,0:T(8,128)}, f32[4,216,768]{2,1,0:T(8,128)}, u32[]{:S(2)}, u32[]{:S(2)}) collective-permute-start(f32[4,216,768]{2,1,0:T(8,128)} %pad_maximum_fusion.2.refs_5_.refs_0_), channel_id=1, source_target_pairs={{0,4},{1,5},{2,6},{3,7},{4,0},{5,1},{6,2},{7,3},{8,12},{9,13},{10,... | collective-permute-start | bytes 7962632 | tf_op jit(solution)/shard_map/ppermute | solution.py:392
  156.0 23.5 %collective-permute-start.19 = (f32[4,72,768]{2,1,0:T(8,128)}, f32[4,72,768]{2,1,0:T(8,128)}, u32[]{:S(2)}, u32[]{:S(2)}) collective-permute-start(f32[4,72,768]{2,1,0:T(8,128)} %pad_maximum_fusion.11.refs_0_), channel_id=1, source_target_pairs={{0,4},{1,5},{2,6},{3,7},{4,0},{5,1},{6,2},{7,3},{8,12},{9,13},{10,... | collective-permute-start | bytes 2654216 | tf_op jit(solution)/shard_map/ppermute | solution.py:392
  167.5 23.5 %collective-permute-start.23 = (f32[4,72,768]{2,1,0:T(8,128)S(1)}, f32[4,72,768]{2,1,0:T(8,128)S(1)}, u32[]{:S(2)}, u32[]{:S(2)}) collective-permute-start(f32[4,72,768]{2,1,0:T(8,128)S(1)} %pad_maximum_fusion.12.refs_0_), channel_id=1, source_target_pairs={{0,4},{1,5},{2,6},{3,7},{4,0},{5,1},{6,2},{7,3},{8,12},{9,13},{10,... | collective-permute-start | bytes 2654216 | tf_op jit(solution)/shard_map/ppermute | solution.py:392
  325.8 35.6 %collective-permute-start.33 = (f32[4,96,1728]{2,1,0:T(8,128)}, f32[4,96,1728]{2,1,0:T(8,128)}, u32[]{:S(2)}, u32[]{:S(2)}) collective-permute-start(f32[4,96,1728]{2,1,0:T(8,128)} %get-tuple-element.194), channel_id=1, source_target_pairs={{0,4},{1,5},{2,6},{3,7},{4,0},{5,1},{6,2},{7,3},{8,12},{9,13},{10,... | collective-permute-start | bytes 7962632 | tf_op jit(solution)/shard_map/ppermute | solution.py:392
  365.5 25.9 %collective-permute-start.34 = (f32[2,96,1728]{2,1,0:T(8,128)}, f32[2,96,1728]{2,1,0:T(8,128)}, u32[]{:S(2)}, u32[]{:S(2)}) collective-permute-start(f32[2,96,1728]{2,1,0:T(8,128)} %pad_maximum_fusion.4), channel_id=1, source_target_pairs={{0,16},{1,17},{2,18},{3,19},{4,12},{5,13},{6,14},{7,15},{8,24},{9,... | collective-permute-start | bytes 3981320 | tf_op jit(solution)/shard_map/ppermute | solution.py:392
  366.8 22.6 %collective-permute-start.28 = (f32[2,96,576]{2,1,0:T(8,128)S(1)}, f32[2,96,576]{2,1,0:T(8,128)}, u32[]{:S(2)}, u32[]{:S(2)}) collective-permute-start(f32[2,96,576]{2,1,0:T(8,128)S(1)} %copy.97), channel_id=1, source_target_pairs={{0,16},{1,17},{2,18},{3,19},{4,12},{5,13},{6,14},{7,15},{8,24},{9,... | collective-permute-start | bytes 1327112 | tf_op jit(solution)/shard_map/ppermute | solution.py:392
  390.7 16.6 %collective-permute-start.29 = (f32[1,96,576]{1,2,0:T(8,128)S(1)}, f32[1,96,576]{1,2,0:T(8,128)S(1)}, u32[]{:S(2)}, u32[]{:S(2)}) collective-permute-start(f32[1,96,576]{1,2,0:T(8,128)S(1)} %slice.185), channel_id=1, source_target_pairs={{0,8},{1,9},{2,10},{3,11},{4,20},{5,21},{6,22},{7,23},{8,0},{9,1},... | collective-permute-start | bytes 663560 | tf_op jit(solution)/shard_map/ppermute | solution.py:392
  392.9 17.3 %collective-permute-start.35 = (f32[1,96,1728]{2,1,0:T(8,128)S(1)}, f32[1,96,1728]{2,1,0:T(8,128)S(1)}, u32[]{:S(2)}, u32[]{:S(2)}) collective-permute-start(f32[1,96,1728]{2,1,0:T(8,128)S(1)} %slice.201), channel_id=1, source_target_pairs={{0,8},{1,9},{2,10},{3,11},{4,20},{5,21},{6,22},{7,23},{8,0},{9,1},... | collective-permute-start | bytes 1990664 | tf_op jit(solution)/shard_map/ppermute | solution.py:392
  409.6 18.5 %collective-permute-start.30 = (f32[1,96,576]{1,2,0:T(8,128)S(1)}, f32[1,96,576]{1,2,0:T(8,128)S(1)}, u32[]{:S(2)}, u32[]{:S(2)}) collective-permute-start(f32[1,96,576]{1,2,0:T(8,128)S(1)} %bitcast.80), channel_id=1, source_target_pairs={{0,8},{1,9},{2,10},{3,11},{4,20},{5,21},{6,22},{7,23},{8,0},{9,1},... | collective-permute-start | bytes 663560 | tf_op jit(solution)/shard_map/ppermute | solution.py:392
  413.9 15.7 %collective-permute-start.36 = (f32[1,96,1728]{2,1,0:T(8,128)S(1)}, f32[1,96,1728]{2,1,0:T(8,128)S(1)}, u32[]{:S(2)}, u32[]{:S(2)}) collective-permute-start(f32[1,96,1728]{2,1,0:T(8,128)S(1)} %bitcast.74), channel_id=1, source_target_pairs={{0,8},{1,9},{2,10},{3,11},{4,20},{5,21},{6,22},{7,23},{8,0},{9,1},... | collective-permute-start | bytes 1990664 | tf_op jit(solution)/shard_map/ppermute | solution.py:392
  429.1 47.7 %collective-permute-start.31 = (f32[2,96,576]{2,1,0:T(8,128)}, f32[2,96,576]{2,1,0:T(8,128)}, u32[]{:S(2)}, u32[]{:S(2)}) collective-permute-start(f32[2,96,576]{2,1,0:T(8,128)} %copy.100), channel_id=1, source_target_pairs={{0,16},{1,17},{2,18},{3,19},{4,12},{5,13},{6,14},{7,15},{8,24},{9,... | collective-permute-start | bytes 1327112 | tf_op jit(solution)/shard_map/ppermute | solution.py:392
  430.9 63.8 %collective-permute-start.37 = (f32[2,96,1728]{2,1,0:T(8,128)}, f32[2,96,1728]{2,1,0:T(8,128)S(1)}, u32[]{:S(2)}, u32[]{:S(2)}) collective-permute-start(f32[2,96,1728]{2,1,0:T(8,128)} %pad_maximum_fusion.5), channel_id=1, source_target_pairs={{0,16},{1,17},{2,18},{3,19},{4,12},{5,13},{6,14},{7,15},{8,24},{9,... | collective-permute-start | bytes 3981320 | tf_op jit(solution)/shard_map/ppermute | solution.py:392
  457.2 16.0 %collective-permute-start.25 = (f32[4,768]{1,0:T(4,128)S(1)}, f32[4,768]{1,0:T(4,128)}, u32[]{:S(2)}, u32[]{:S(2)}) collective-permute-start(f32[4,768]{1,0:T(4,128)S(1)} %fusion.7), channel_id=1, source_target_pairs={{0,8},{1,9},{2,10},{3,11},{4,12},{5,13},{6,14},{7,15},{8,0},{9,1},... | collective-permute-start | bytes 36872 | tf_op jit(solution)/shard_map/ppermute | solution.py:471
  479.1 22.6 %collective-permute-start.32 = (f32[4,96,576]{2,1,0:T(8,128)}, f32[4,96,576]{2,1,0:T(8,128)}, u32[]{:S(2)}, u32[]{:S(2)}) collective-permute-start(f32[4,96,576]{2,1,0:T(8,128)} %pad_maximum_fusion.9), channel_id=1, source_target_pairs={{0,4},{1,5},{2,6},{3,7},{4,0},{5,1},{6,2},{7,3},{8,12},{9,13},{10,... | collective-permute-start | bytes 2654216 | tf_op jit(solution)/shard_map/ppermute | solution.py:392
  496.7 25.4 %collective-permute-start.38 = (f32[4,96,1728]{2,1,0:T(8,128)}, f32[4,96,1728]{2,1,0:T(8,128)}, u32[]{:S(2)}, u32[]{:S(2)}) collective-permute-start(f32[4,96,1728]{2,1,0:T(8,128)} %pad_maximum_fusion), channel_id=1, source_target_pairs={{0,4},{1,5},{2,6},{3,7},{4,0},{5,1},{6,2},{7,3},{8,12},{9,13},{10,... | collective-permute-start | bytes 7962632 | tf_op jit(solution)/shard_map/ppermute | solution.py:392
  (59 other events, 600.5 us)
